TPU v7x, 32 devices: a whole 2x2x4 slice. The times are simulated.
32 devices in a mesh: dp: 8 (over y, x, core), seq: 4 (over z).
Axes of the slice: x: 2, y: 2, z: 4, core: 2. Of those that a mesh axis runs over, the one named last changes fastest.
Arguments:
- hidden_states: bfloat16 [4096, 5120], P(('dp', 'seq')), may hold values from -6 to 6
- value_weight: bfloat16 [5120, 1024], P('dp'), may hold values from -0.078125 to 0.078125
- query_states: bfloat16 [4096, 8192], P(('dp', 'seq')), may hold values from -140 to 140
- key_states: bfloat16 [4096, 1024], P(('dp', 'seq')), may hold values from -4.5 to 4.5
- cotangent: bfloat16 [4096, 8192], P(('dp', 'seq')), may hold values from -6 to 6
- lengths: int32 [8, 8], P('dp'), may hold values from 1 to 256, 512 in all within a row
Outputs:
- attention_out: bfloat16 [4096, 8192], P(('dp', 'seq'))
- query_grad: bfloat16 [4096, 8192], P(('dp', 'seq'))
- key_grad: bfloat16 [4096, 1024], P(('dp', 'seq'))
- input_grad: bfloat16 [4096, 5120], P(('dp', 'seq'))
- value_weight_grad: float32 [5120, 1024], P('dp')
Inputs may be any that keep to these rules, and one draw needn't show every extreme that they name: Row g lists the 8 response lengths of group g's pack; they sum to 512 and the longest is 256.
All inputs are finite; a program needn't handle non-finite values.
Results may differ from a plain program's by a relative error of at most 0.04.
Values may be sent and summed in bfloat16 or wider, within the bound.
A program may use at most 256 MiB of HBM per device.

v0:
```python
import functools
import math

import jax
import jax.numpy as jnp
from jax import lax
from jax.experimental import pallas as pl
from jax.experimental.pallas import tpu as pltpu
from jax.sharding import PartitionSpec as P

HEADS = 64
KV_HEADS = 8
HEAD_DIM = 128
GROUP = HEADS // KV_HEADS
SCALE = HEAD_DIM ** (-0.5)
MESH = pl.DeviceIdType.MESH
BF = jnp.bfloat16
F32 = jnp.float32
PARTS = 4
AR_CUTS = 2

NT = (((1,), (1,)), ((), ()))


def mm(a, b, dims=(((1,), (0,)), ((), ()))):
    return lax.dot_general(a, b, dims, preferred_element_type=F32)


def kernel(
    n, seq, back, tok, depth, start_ref, hid, weight, query, keys, cot,
    out, dq, dk, ig, dw,
    hbuf, ht, wv, qv, cv, ov, dqv, kwin, vwin, pbuf, prec, csum, vrec,
    dpart, dsend, drec, dvall, igacc, igs, dwv, msg, rec_out, rec_in, tot,
    loc, hs, hr, ks, kr, ps, pr, vs, vr, vcs, vcr, ds_, dr, gs, gr, fs, fr, igss, igr,
    ais, air, aos, aor, osem, dwsem,
):
    chips = n // 2
    kv_cols = KV_HEADS * HEAD_DIM
    cols = kv_cols // PARTS
    heads_per = KV_HEADS // PARTS
    window = (back + 1) * tok
    d = lax.axis_index("dp")
    z = lax.axis_index("seq")
    c = lax.div(d, 2)
    k = lax.rem(d, 2)
    other = 1 - k
    partner = c * 2 + other
    pending = []

    def remote(src, dst, ssem, rsem, **where):
        return pltpu.make_async_remote_copy(
            src_ref=src, dst_ref=dst, send_sem=ssem, recv_sem=rsem,
            device_id=where, device_id_type=MESH,
        )

    def when(cond, fn):
        if cond is None:
            fn()
        else:
            pl.when(cond)(fn)

    def start(copy, cond=None):
        when(cond, lambda: copy.start())
        pending.append((cond, copy))

    kwin[pl.ds(0, back)] = jnp.zeros((back, tok, kv_cols), BF)
    vwin[:, pl.ds(0, back)] = jnp.zeros((PARTS, back, tok, cols), BF)

    barrier = pltpu.get_barrier_semaphore()
    for off in range(1, n):
        pl.semaphore_signal(barrier, 1, device_id={"dp": lax.rem(d + off, n)}, device_id_type=MESH)

    @pl.when(z > 0)
    def _():
        pl.semaphore_signal(barrier, 1, device_id={"seq": z - 1}, device_id_type=MESH)

    @pl.when(z < seq - 1)
    def _():
        pl.semaphore_signal(barrier, 1, device_id={"seq": z + 1}, device_id_type=MESH)

    def chunk(p):
        if depth % 128 == 0:
            return hid.at[:, pl.ds(pl.multiple_of(p * depth, 128), depth)]
        return hid.at[p]

    local = [
        pltpu.make_async_copy(chunk(d), hbuf.at[k, c], loc.at[0]),
        pltpu.make_async_copy(weight, wv, loc.at[1]),
        pltpu.make_async_copy(keys, kwin.at[back], loc.at[2]),
        pltpu.make_async_copy(query, qv, loc.at[3]),
        pltpu.make_async_copy(cot, cv, loc.at[4]),
    ]
    for copy in local:
        copy.start()
    inner = jnp.logical_and(z > 0, z < seq - 1)
    pl.semaphore_wait(barrier, n - 1 + jnp.where(inner, 2, 1))

    for off in range(n - 1, 0, -1):
        p = lax.rem(d + off, n)
        start(remote(chunk(p), hbuf.at[k, c], hs.at[off], hr.at[k, c], dp=p))

    def key_hop(s):
        src = keys if s == 1 else kwin.at[back - s + 1]
        cond = jnp.logical_and(z < seq - 1, z - s + 1 >= 0)
        start(remote(src, kwin.at[back - s], ks.at[s - 1], kr.at[s - 1], seq=z + 1), cond)

    def key_land(s):
        @pl.when(z - s >= 0)
        def _():
            remote(keys, kwin.at[back - s], ks.at[s - 1], kr.at[s - 1], seq=z).wait_recv()

    key_hop(1)
    local[0].wait()
    local[1].wait()

    def hidden_land(kk):
        for cc in range(chips):
            @pl.when(jnp.logical_or(cc != c, kk != k))
            def _():
                remote(hbuf.at[kk, cc], hbuf.at[kk, cc], hs.at[0], hr.at[kk, cc], dp=d).wait_recv()

    def partial_values(kk, gi):
        rows = hbuf[kk].reshape(chips * tok, depth)
        got = mm(rows, wv[:, gi * cols:(gi + 1) * cols])
        pbuf[gi, kk] = got.astype(BF).reshape(chips, tok, cols)

    hidden_land(other)
    for gi in range(PARTS):
        partial_values(other, gi)
        start(remote(pbuf.at[gi, other], prec.at[gi], ps.at[gi], pr.at[gi], dp=partner))
    hidden_land(k)
    for gi in range(PARTS):
        partial_values(k, gi)
    for gi in range(PARTS):
        remote(pbuf.at[gi, k], prec.at[gi], ps.at[gi], pr.at[gi], dp=partner).wait_recv()
        csum[gi] = (pbuf[gi, k].astype(F32) + prec[gi].astype(F32)).astype(BF)
        for co in range(1, chips):
            cc = lax.rem(c + co, chips)
            start(remote(
                csum.at[gi, cc], vrec.at[gi, c], vs.at[gi, co], vr.at[gi, c], dp=cc * 2 + k
            ))

    for s in range(2, back + 1):
        key_land(s - 1)
        key_hop(s)

    for kk in range(2):
        for cc in range(chips):
            ht[:, (kk * chips + cc) * tok:(kk * chips + cc + 1) * tok] = hbuf[kk, cc].T

    def value_hop(gi, s):
        cond = jnp.logical_and(z < seq - 1, z - s + 1 >= 0)
        start(remote(
            vwin.at[gi, back - s + 1], vwin.at[gi, back - s],
            vcs.at[gi, s - 1], vcr.at[gi, s - 1], seq=z + 1,
        ), cond)

    def value_land(gi, s):
        @pl.when(z - s >= 0)
        def _():
            remote(
                vwin.at[gi, back - s], vwin.at[gi, back - s],
                vcs.at[gi, s - 1], vcr.at[gi, s - 1], seq=z,
            ).wait_recv()

    def values_done(gi):
        total = csum[gi, c].astype(F32)
        for co in range(1, chips):
            cc = lax.rem(c + co, chips)
            remote(
                vrec.at[gi, cc], vrec.at[gi, cc], vs.at[gi, 0], vr.at[gi, cc], dp=d
            ).wait_recv()
            total += vrec[gi, cc].astype(F32)
        vwin[gi, back] = total.astype(BF)
        value_hop(gi, 1)

    def values_on(gi):
        for s in range(2, back + 1):
            value_land(gi, s - 1)
            value_hop(gi, s)

    def attention(gi):
        value_land(gi, back)
        key_at = (z - back) * tok + lax.broadcasted_iota(jnp.int32, (window, tok), 0)
        query_at = z * tok + lax.broadcasted_iota(jnp.int32, (window, tok), 1)
        first = start_ref[...]
        mask = jnp.logical_and(key_at >= first, key_at <= query_at)
        bias = jnp.where(mask, 0.0, -1e30).astype(F32)
        bias = jnp.concatenate([bias, bias], axis=1)

        def one(jl, carry):
            j = gi * heads_per + jl
            kcol = pl.ds(pl.multiple_of(j * HEAD_DIM, HEAD_DIM), HEAD_DIM)
            lcol = pl.ds(pl.multiple_of(jl * HEAD_DIM, HEAD_DIM), HEAD_DIM)
            kj = kwin[:, :, kcol].reshape(window, HEAD_DIM)
            vj = vwin[gi, :, :, lcol].reshape(window, HEAD_DIM)
            kt = kj.T
            vt = vj.T
            dkj = jnp.zeros((window, HEAD_DIM), F32)
            dvj = jnp.zeros((window, HEAD_DIM), F32)
            for pair in range(GROUP // 2):
                at = [
                    pl.ds(
                        pl.multiple_of((j * GROUP + pair * 2 + h) * HEAD_DIM, HEAD_DIM), HEAD_DIM
                    )
                    for h in range(2)
                ]
                qp = jnp.concatenate([qv[:, a] for a in at], axis=0)
                cp = jnp.concatenate([cv[:, a] for a in at], axis=0)
                st = mm(kj, qp, NT) * (SCALE * math.log2(math.e)) + bias
                dp = mm(vj, cp, NT)
                e = jnp.exp2(st - jnp.max(st, axis=0, keepdims=True))
                p = e * (1.0 / jnp.sum(e, axis=0, keepdims=True))
                pb = p.astype(BF)
                delta = jnp.sum(p * dp, axis=0, keepdims=True)
                sg = (p * (dp - delta)).astype(BF)
                dvj += mm(pb, cp)
                dkj += mm(sg, qp)
                ot = mm(vt, pb)
                qt = mm(kt, sg) * SCALE
                for h in range(2):
                    part = slice(h * HEAD_DIM, (h + 1) * HEAD_DIM)
                    ov[:, at[h]] = ot[:, part].T.astype(BF)
                    dqv[:, at[h]] = qt[:, part].T.astype(BF)
            dpart[0, gi, :, :, lcol] = dvj.reshape(back + 1, tok, HEAD_DIM)
            dpart[1, gi, :, :, lcol] = (dkj * SCALE).reshape(back + 1, tok, HEAD_DIM)
            return carry

        lax.fori_loop(0, heads_per, one, 0)
        wide = heads_per * GROUP * HEAD_DIM
        mine = pl.ds(gi * wide, wide)
        for index, (a, b) in enumerate(((ov, out), (dqv, dq))):
            copy = pltpu.make_async_copy(a.at[:, mine], b.at[:, mine], osem.at[gi, index])
            copy.start()
            pending.append((None, copy))

    def grad_copy(w, gi, i):
        return remote(
            dsend.at[w, gi, i], drec.at[w, gi, i], ds_.at[w, gi, i], dr.at[w, gi, i], seq=z - 1
        )

    def grad_step(w, gi, i):
        if i >= 1:
            @pl.when(jnp.logical_and(z < seq - 1, z - back + i >= 0))
            def _():
                grad_copy(w, gi, i - 1).wait_recv()
                dpart[w, gi, i] += drec[w, gi, i - 1].astype(F32)
        if i < back:
            dsend[w, gi, i] = dpart[w, gi, i].astype(BF)
            start(grad_copy(w, gi, i), z - back + i >= 0)

    def gather_send(gi):
        grad_step(0, gi, back)
        dvall[gi, k, c] = dpart[0, gi, back].astype(BF)
        for co in range(1, chips):
            cc = lax.rem(c + co, chips)
            start(remote(
                dvall.at[gi, k, c], dvall.at[gi, k, c], gs.at[gi, co], gr.at[gi, k, c], dp=cc * 2 + k
            ))
        start(remote(
            dvall.at[gi, k, c], dvall.at[gi, k, c], fs.at[gi, 0], gr.at[gi, k, c], dp=partner
        ))
        grad_step(1, gi, back)
        dk[:, gi * cols:(gi + 1) * cols] = dpart[1, gi, back].astype(BF)

    def gather_land(gi, kk, cc):
        remote(
            dvall.at[gi, kk, cc], dvall.at[gi, kk, cc], gs.at[gi, 0], gr.at[gi, kk, cc], dp=d
        ).wait_recv()

    def gather_on(gi):
        for co in range(1, chips):
            cc = lax.rem(c + co, chips)
            gather_land(gi, k, cc)
            start(remote(
                dvall.at[gi, k, cc], dvall.at[gi, k, cc], fs.at[gi, co], gr.at[gi, k, cc], dp=partner
            ))

    half = seq // 2
    low = z < half
    inward = jnp.where(low, z + 1, z - 1)
    outward = jnp.where(low, z - 1, z + 1)
    middle = jnp.logical_or(z == half - 1, z == half)
    edge = jnp.logical_or(z == 0, z == seq - 1)
    not_middle = jnp.logical_not(middle)
    not_edge = jnp.logical_not(edge)
    cut = depth // AR_CUTS

    def weight_grad(gi):
        for cc in range(chips):
            gather_land(gi, other, cc)
        rows = dvall[gi].reshape(n * tok, cols)
        dwv[gi] = mm(ht[...], rows)
        for r in range(AR_CUTS):
            reduce_in(gi, r, True)

    def reduce_in(gi, r, first):
        at = (gi, pl.ds(r * cut, cut))

        def send():
            msg[at] = dwv[at].astype(BF)

        if first:
            @pl.when(edge)
            def _():
                send()
            cond = edge
        else:
            @pl.when(not_edge)
            def _():
                remote(msg.at[at], rec_out.at[at], ais.at[gi, r], aor.at[gi, r], seq=z).wait_recv()
                dwv[at] += rec_out[at].astype(F32)
                send()
            cond = not_edge
        a = jnp.logical_and(cond, not_middle)
        b = jnp.logical_and(cond, middle)
        start(remote(msg.at[at], rec_out.at[at], ais.at[gi, r], aor.at[gi, r], seq=inward), a)
        start(remote(msg.at[at], rec_in.at[at], ais.at[gi, r], air.at[gi, r], seq=inward), b)

    def reduce_out(gi, r):
        at = (gi, pl.ds(r * cut, cut))
        remote(msg.at[at], rec_in.at[at], ais.at[gi, r], air.at[gi, r], seq=z).wait_recv()

        @pl.when(middle)
        def _():
            tot[at] = (msg[at].astype(F32) + rec_in[at].astype(F32)).astype(BF)

        @pl.when(not_middle)
        def _():
            tot[at] = rec_in[at]

        start(remote(tot.at[at], rec_in.at[at], aos.at[gi, r], air.at[gi, r], seq=outward), not_edge)
        dwv[at] = tot[at].astype(F32)
        copy = pltpu.make_async_copy(
            dwv.at[at], dw.at[pl.ds(r * cut, cut), pl.ds(gi * cols, cols)], dwsem.at[gi, r]
        )
        copy.start()
        pending.append((None, copy))

    def input_grad(gi):
        rows = dvall[gi].reshape(n * tok, cols)
        got = mm(rows, wv[:, gi * cols:(gi + 1) * cols], NT)
        if gi == 0:
            igacc[...] = got
        elif gi < PARTS - 1:
            igacc[...] += got
        else:
            igs[...] = (igacc[...] + got).astype(BF).reshape(2, chips, tok, depth)
            for off in range(1, n):
                p = lax.rem(d + off, n)
                start(remote(
                    igs.at[lax.rem(p, 2), lax.div(p, 2)], ig.at[k, c],
                    igss.at[off], igr.at[k, c], dp=p,
                ))
            copy = pltpu.make_async_copy(igs.at[k, c], ig.at[k, c], loc.at[5])
            copy.start()
            pending.append((None, copy))

    for gi in range(PARTS):
        values_done(gi)
    local[2].wait()
    local[3].wait()
    local[4].wait()
    key_land(back)

    def grads_start(gi):
        attention(gi)
        grad_step(0, gi, 0)
        grad_step(1, gi, 0)

    def grads_on(gi):
        for i in range(1, back):
            grad_step(0, gi, i)
            grad_step(1, gi, i)

    def reduces(gi):
        for r in range(AR_CUTS):
            reduce_in(gi, r, False)

    def finish(gi):
        for r in range(AR_CUTS):
            reduce_out(gi, r)

    stages = [values_on, grads_start, grads_on, gather_send, gather_on, weight_grad, input_grad, reduces, finish]
    for t in range(PARTS + len(stages) - 1):
        for s in range(len(stages)):
            if 0 <= t - s < PARTS:
                stages[s](t - s)

    for off in range(1, n):
        p = lax.rem(d + off, n)
        slot = (lax.rem(p, 2), lax.div(p, 2))
        remote(igs.at[slot], ig.at[slot], igss.at[0], igr.at[slot], dp=d).wait_recv()
    for cond, copy in pending:
        if hasattr(copy, "wait_send") and copy.is_remote:
            when(cond, lambda copy=copy: copy.wait_send())
        else:
            copy.wait()


def body(hidden_states, value_weight, query_states, key_states, cotangent, lengths, n, seq):
    tok, width = hidden_states.shape
    depth = value_weight.shape[0]
    kv_cols = value_weight.shape[1]
    cols = kv_cols // PARTS
    chips = n // 2
    packed = tok * seq
    back = -(-(packed // 2 - 1) // tok)
    ends = jnp.cumsum(lengths[0])[:-1]
    at = lax.axis_index("seq") * tok + jnp.arange(tok, dtype=jnp.int32)
    first = jnp.max(jnp.where(ends[:, None] <= at[None, :], ends[:, None], 0), axis=0)[None, :]
    hid = hidden_states
    if depth % 128:
        hid = hid.reshape(tok, n, depth).transpose(1, 0, 2)
    vmem = pl.BlockSpec(memory_space=pltpu.VMEM)
    hbm = pl.BlockSpec(memory_space=pl.ANY)
    dma = pltpu.SemaphoreType.DMA
    out, dq, dk, ig, dw = pl.pallas_call(
        functools.partial(kernel, n, seq, back, tok, depth),
        out_shape=(
            jax.ShapeDtypeStruct(query_states.shape, BF),
            jax.ShapeDtypeStruct(query_states.shape, BF),
            jax.ShapeDtypeStruct(key_states.shape, BF),
            jax.ShapeDtypeStruct((2, chips, tok, depth), BF),
            jax.ShapeDtypeStruct((depth, kv_cols), F32),
        ),
        in_specs=[vmem, hbm, hbm, hbm, hbm, hbm],
        out_specs=(hbm, hbm, vmem, hbm, hbm),
        scratch_shapes=[
            pltpu.VMEM((2, chips, tok, depth), BF),
            pltpu.VMEM((depth, n * tok), BF),
            pltpu.VMEM((depth, kv_cols), BF),
            pltpu.VMEM(query_states.shape, BF),
            pltpu.VMEM(query_states.shape, BF),
            pltpu.VMEM(query_states.shape, BF),
            pltpu.VMEM(query_states.shape, BF),
            pltpu.VMEM((back + 1, tok, kv_cols), BF),
            pltpu.VMEM((PARTS, back + 1, tok, cols), BF),
            pltpu.VMEM((PARTS, 2, chips, tok, cols), BF),
            pltpu.VMEM((PARTS, chips, tok, cols), BF),
            pltpu.VMEM((PARTS, chips, tok, cols), BF),
            pltpu.VMEM((PARTS, chips, tok, cols), BF),
            pltpu.VMEM((2, PARTS, back + 1, tok, cols), F32),
            pltpu.VMEM((2, PARTS, back, tok, cols), BF),
            pltpu.VMEM((2, PARTS, back, tok, cols), BF),
            pltpu.VMEM((PARTS, 2, chips, tok, cols), BF),
            pltpu.VMEM((n * tok, depth), F32),
            pltpu.VMEM((2, chips, tok, depth), BF),
            pltpu.VMEM((PARTS, depth, cols), F32),
            pltpu.VMEM((PARTS, depth, cols), BF),
            pltpu.VMEM((PARTS, depth, cols), BF),
            pltpu.VMEM((PARTS, depth, cols), BF),
            pltpu.VMEM((PARTS, depth, cols), BF),
            dma((6,)),
            dma((n,)), dma((2, chips)),
            dma((back,)), dma((back,)),
            dma((PARTS,)), dma((PARTS,)),
            dma((PARTS, chips)), dma((PARTS, chips)),
            dma((PARTS, back)), dma((PARTS, back)),
            dma((2, PARTS, back)), dma((2, PARTS, back)),
            dma((PARTS, chips)), dma((PARTS, 2, chips)),
            dma((PARTS, chips)), dma((1,)),
            dma((n,)), dma((2, chips)),
            dma((PARTS, AR_CUTS)), dma((PARTS, AR_CUTS)),
            dma((PARTS, AR_CUTS)), dma((PARTS, AR_CUTS)),
            dma((PARTS, 2)), dma((PARTS, AR_CUTS)),
        ],
        compiler_params=pltpu.CompilerParams(
            collective_id=0, has_side_effects=True, vmem_limit_bytes=60 * 1024 * 1024
        ),
    )(first, hid, value_weight, query_states, key_states, cotangent)
    input_grad = ig.transpose(2, 1, 0, 3).reshape(tok, width)
    return out, dq, dk, input_grad, dw


def solution(mesh):
    rows = P(("dp", "seq"), None)
    placed = (rows, P("dp", None), rows, rows, rows, P("dp", None))
    return jax.shard_map(
        functools.partial(body, n=mesh.shape["dp"], seq=mesh.shape["seq"]),
        mesh=mesh,
        in_specs=placed,
        out_specs=(rows, rows, rows, rows, P("dp", None)),
        check_vma=False,
    )
```

profile of v0, /device:TPU:0, one launch (start us, length us, event | category | flops | bytes accessed | tf_op | source)
XLA Modules:
  0.0 127.2 jit_solution(6404644402875936088)
XLA Ops:
  0.6 0.8 reduce-window.4
  1.5 0.6 select_reduce_fusion
  2.1 115.2 %shard_map.101 = (bf16[128,8192]{1,0:T(8,128)(2,1)}, bf16[128,8192]{1,0:T(8,128)(2,1)}, bf16[128,1024]{1,0:T(8,128)(2,1)}, bf16[2,4,128,640]{3,2,1,0:T(8,128)(2,1)}, f32[640,1024]{1,0:T(8,128)}) custom-call(s32[1,128]{1,0:T(1,128)} %bitcast.8, bf16[128,5120]{1,0:T(8,128)(2,1)} %hid.1, bf16[640,1024]{1,0:T(8,128)(2,1)} %weight.1, bf16[128,8192]{1,0:T(8,128)(2,1)} %query.1, ...), custom_call_target="tpu_custom_call" | custom-call | tf_op jit(solution)/shard_map/pallas_call | solution.py:418
  117.3 0.0 copy-start.2
  117.3 1.9 %copy.13 = bf16[128,4,2,640]{0,3,2,1:T(8,128)(2,1)S(1)} copy(bf16[128,4,2,640]{3,0,1,2:T(8,128)(2,1)} %bitcast.7) | data formatting | bytes 2621440 | tf_op jit(solution)/shard_map/transpose | solution.py:472
  119.3 1.4 %copy.14 = bf16[128,5120]{1,0:T(8,128)(2,1)} copy(bf16[128,5120]{0,1:T(8,128)(2,1)S(1)} %bitcast.6) | data formatting | bytes 2621440
  120.7 0.0 copy-done.2
  120.7 0.0 copy-start.1
  120.7 1.3 %copy.19 = bf16[128,8192]{1,0:T(8,128)(2,1)} copy(bf16[128,8192]{1,0:T(8,128)(2,1)S(1)} %copy-done.2) | data formatting | bytes 4194304
  122.0 1.0 copy-done.1
  123.1 0.0 copy-start.3
  123.1 0.0 copy-start
  123.1 1.3 %copy.20 = bf16[128,8192]{1,0:T(8,128)(2,1)} copy(bf16[128,8192]{1,0:T(8,128)(2,1)S(1)} %copy-done.1) | data formatting | bytes 4194304
  124.4 0.0 copy-done.3
  124.4 0.7 copy.21
  125.1 0.7 copy-done
  125.7 1.5 %copy.22 = f32[640,1024]{1,0:T(8,128)} copy(f32[640,1024]{1,0:T(8,128)S(1)} %copy-done) | data formatting | bytes 5242880
  (2 shorter events, 0.0 us)
Async XLA Ops:
  117.3 3.4 %copy-start.2 = (bf16[128,8192]{1,0:T(8,128)(2,1)S(1)}, bf16[128,8192]{1,0:T(8,128)(2,1)}, u32[]{:S(2)}) copy-start(bf16[128,8192]{1,0:T(8,128)(2,1)} %get-tuple-element.30) | copy-start | bytes 6291460
  120.7 2.3 %copy-start.1 = (bf16[128,8192]{1,0:T(8,128)(2,1)S(1)}, bf16[128,8192]{1,0:T(8,128)(2,1)}, u32[]{:S(2)}) copy-start(bf16[128,8192]{1,0:T(8,128)(2,1)} %get-tuple-element.31) | copy-start | bytes 6291460
  123.1 1.3 %copy-start.3 = (bf16[128,1024]{1,0:T(8,128)(2,1)S(1)}, bf16[128,1024]{1,0:T(8,128)(2,1)}, u32[]{:S(2)}) copy-start(bf16[128,1024]{1,0:T(8,128)(2,1)} %get-tuple-element.32) | copy-start | bytes 786436
  123.1 2.7 %copy-start = (f32[640,1024]{1,0:T(8,128)S(1)}, f32[640,1024]{1,0:T(8,128)}, u32[]{:S(2)}) copy-start(f32[640,1024]{1,0:T(8,128)} %get-tuple-element.34) | copy-start | bytes 7864324
where the time goes:
time: 127 us
  Pallas kernels  115 us (91%)
  local copies, waits for them, and re-layouts  9.9 us (8%)
  other arithmetic  1.43 us (1%)
    pallas_call x1, Pallas kernels, body(): pl.pallas_call(functools.partial(kernel, n, seq, back, tok, depth), out_s...  115 us
    unnamed x13, local copies, waits for them, and re-layouts  7.97 us

commit v1 on v0

--- a/solution.py
+++ b/solution.py
@@ -27,9 +27,9 @@
 
 
 def kernel(
-    n, seq, back, tok, depth, start_ref, hid, weight, query, keys, cot,
+    n, seq, back, tok, depth, lengths, hid, weight, query, keys, cot,
     out, dq, dk, ig, dw,
-    hbuf, ht, wv, qv, cv, ov, dqv, kwin, vwin, pbuf, prec, csum, vrec,
+    hbuf, ht, wv, qv, cv, ov, dqv, kwin, vwin, probs, pbuf, prec, csum, vrec,
     dpart, dsend, drec, dvall, igacc, igs, dwv, msg, rec_out, rec_in, tot,
     loc, hs, hr, ks, kr, ps, pr, vs, vr, vcs, vcr, ds_, dr, gs, gr, fs, fr, igss, igr,
     ais, air, aos, aor, osem, dwsem,
@@ -63,7 +63,7 @@
         when(cond, lambda: copy.start())
         pending.append((cond, copy))
 
-    kwin[pl.ds(0, back)] = jnp.zeros((back, tok, kv_cols), BF)
+    kwin[:, pl.ds(0, back)] = jnp.zeros((PARTS, back, tok, cols), BF)
     vwin[:, pl.ds(0, back)] = jnp.zeros((PARTS, back, tok, cols), BF)
 
     barrier = pltpu.get_barrier_semaphore()
@@ -86,32 +86,42 @@
     local = [
         pltpu.make_async_copy(chunk(d), hbuf.at[k, c], loc.at[0]),
         pltpu.make_async_copy(weight, wv, loc.at[1]),
-        pltpu.make_async_copy(keys, kwin.at[back], loc.at[2]),
-        pltpu.make_async_copy(query, qv, loc.at[3]),
-        pltpu.make_async_copy(cot, cv, loc.at[4]),
+        pltpu.make_async_copy(query, qv, loc.at[2]),
+        pltpu.make_async_copy(cot, cv, loc.at[3]),
+    ] + [
+        pltpu.make_async_copy(keys.at[:, pl.ds(gi * cols, cols)], kwin.at[gi, back], loc.at[5 + gi])
+        for gi in range(PARTS)
     ]
     for copy in local:
         copy.start()
     inner = jnp.logical_and(z > 0, z < seq - 1)
     pl.semaphore_wait(barrier, n - 1 + jnp.where(inner, 2, 1))
 
+    def key_hop(gi, s):
+        src = keys.at[:, pl.ds(gi * cols, cols)] if s == 1 else kwin.at[gi, back - s + 1]
+        cond = jnp.logical_and(z < seq - 1, z - s + 1 >= 0)
+        start(remote(
+            src, kwin.at[gi, back - s], ks.at[gi, s - 1], kr.at[gi, s - 1], seq=z + 1
+        ), cond)
+
+    def key_land(gi, s):
+        @pl.when(z - s >= 0)
+        def _():
+            remote(
+                kwin.at[gi, back - s], kwin.at[gi, back - s],
+                ks.at[gi, s - 1], kr.at[gi, s - 1], seq=z,
+            ).wait_recv()
+
+    def keys_on(gi):
+        for s in range(2, back + 1):
+            key_land(gi, s - 1)
+            key_hop(gi, s)
+
+    for gi in range(PARTS):
+        key_hop(gi, 1)
     for off in range(n - 1, 0, -1):
         p = lax.rem(d + off, n)
         start(remote(chunk(p), hbuf.at[k, c], hs.at[off], hr.at[k, c], dp=p))
-
-    def key_hop(s):
-        src = keys if s == 1 else kwin.at[back - s + 1]
-        cond = jnp.logical_and(z < seq - 1, z - s + 1 >= 0)
-        start(remote(src, kwin.at[back - s], ks.at[s - 1], kr.at[s - 1], seq=z + 1), cond)
-
-    def key_land(s):
-        @pl.when(z - s >= 0)
-        def _():
-            remote(keys, kwin.at[back - s], ks.at[s - 1], kr.at[s - 1], seq=z).wait_recv()
-
-    key_hop(1)
-    local[0].wait()
-    local[1].wait()
 
     def hidden_land(kk):
         for cc in range(chips):
@@ -124,14 +134,20 @@
         got = mm(rows, wv[:, gi * cols:(gi + 1) * cols])
         pbuf[gi, kk] = got.astype(BF).reshape(chips, tok, cols)
 
-    hidden_land(other)
-    for gi in range(PARTS):
-        partial_values(other, gi)
-        start(remote(pbuf.at[gi, other], prec.at[gi], ps.at[gi], pr.at[gi], dp=partner))
-    hidden_land(k)
-    for gi in range(PARTS):
-        partial_values(k, gi)
-    for gi in range(PARTS):
+    def values_pair():
+        local[0].wait()
+        local[1].wait()
+        hidden_land(other)
+        for gi in range(PARTS):
+            partial_values(other, gi)
+            start(remote(pbuf.at[gi, other], prec.at[gi], ps.at[gi], pr.at[gi], dp=partner))
+
+    def values_own():
+        hidden_land(k)
+        for gi in range(PARTS):
+            partial_values(k, gi)
+
+    def values_send(gi):
         remote(pbuf.at[gi, k], prec.at[gi], ps.at[gi], pr.at[gi], dp=partner).wait_recv()
         csum[gi] = (pbuf[gi, k].astype(F32) + prec[gi].astype(F32)).astype(BF)
         for co in range(1, chips):
@@ -140,13 +156,10 @@
                 csum.at[gi, cc], vrec.at[gi, c], vs.at[gi, co], vr.at[gi, c], dp=cc * 2 + k
             ))
 
-    for s in range(2, back + 1):
-        key_land(s - 1)
-        key_hop(s)
-
-    for kk in range(2):
-        for cc in range(chips):
-            ht[:, (kk * chips + cc) * tok:(kk * chips + cc + 1) * tok] = hbuf[kk, cc].T
+    def turn_hidden():
+        for kk in range(2):
+            for cc in range(chips):
+                ht[:, (kk * chips + cc) * tok:(kk * chips + cc + 1) * tok] = hbuf[kk, cc].T
 
     def value_hop(gi, s):
         cond = jnp.logical_and(z < seq - 1, z - s + 1 >= 0)
@@ -179,60 +192,74 @@
             value_land(gi, s - 1)
             value_hop(gi, s)
 
-    def attention(gi):
-        value_land(gi, back)
+    def pair_rows(j, pair):
+        at = [slice((j * GROUP + pair * 2 + h) * HEAD_DIM, (j * GROUP + pair * 2 + h + 1) * HEAD_DIM)
+              for h in range(2)]
+        qp = jnp.concatenate([qv[:, a] for a in at], axis=0)
+        cp = jnp.concatenate([cv[:, a] for a in at], axis=0)
+        return at, qp, cp
+
+    def scores(gi):
+        local[5 + gi - 1].wait()
+        key_land(gi, back)
         key_at = (z - back) * tok + lax.broadcasted_iota(jnp.int32, (window, tok), 0)
         query_at = z * tok + lax.broadcasted_iota(jnp.int32, (window, tok), 1)
-        first = start_ref[...]
+        own_at = z * tok + lax.broadcasted_iota(jnp.int32, (1, tok), 1)
+        first = jnp.zeros((1, tok), jnp.int32)
+        end = 0
+        for r in range(lengths.shape[1] - 1):
+            end = end + lengths[0, r]
+            first = jnp.where(own_at >= end, end, first)
         mask = jnp.logical_and(key_at >= first, key_at <= query_at)
         bias = jnp.where(mask, 0.0, -1e30).astype(F32)
         bias = jnp.concatenate([bias, bias], axis=1)
-
-        def one(jl, carry):
+        for jl in range(heads_per):
             j = gi * heads_per + jl
-            kcol = pl.ds(pl.multiple_of(j * HEAD_DIM, HEAD_DIM), HEAD_DIM)
-            lcol = pl.ds(pl.multiple_of(jl * HEAD_DIM, HEAD_DIM), HEAD_DIM)
-            kj = kwin[:, :, kcol].reshape(window, HEAD_DIM)
-            vj = vwin[gi, :, :, lcol].reshape(window, HEAD_DIM)
-            kt = kj.T
-            vt = vj.T
-            dkj = jnp.zeros((window, HEAD_DIM), F32)
+            lcol = slice(jl * HEAD_DIM, (jl + 1) * HEAD_DIM)
+            kj = kwin[gi, :, :, lcol].reshape(window, HEAD_DIM)
             dvj = jnp.zeros((window, HEAD_DIM), F32)
             for pair in range(GROUP // 2):
-                at = [
-                    pl.ds(
-                        pl.multiple_of((j * GROUP + pair * 2 + h) * HEAD_DIM, HEAD_DIM), HEAD_DIM
-                    )
-                    for h in range(2)
-                ]
-                qp = jnp.concatenate([qv[:, a] for a in at], axis=0)
-                cp = jnp.concatenate([cv[:, a] for a in at], axis=0)
+                at, qp, cp = pair_rows(j, pair)
                 st = mm(kj, qp, NT) * (SCALE * math.log2(math.e)) + bias
-                dp = mm(vj, cp, NT)
                 e = jnp.exp2(st - jnp.max(st, axis=0, keepdims=True))
-                p = e * (1.0 / jnp.sum(e, axis=0, keepdims=True))
-                pb = p.astype(BF)
-                delta = jnp.sum(p * dp, axis=0, keepdims=True)
-                sg = (p * (dp - delta)).astype(BF)
+                pb = (e * (1.0 / jnp.sum(e, axis=0, keepdims=True))).astype(BF)
+                probs[j, pair] = pb
                 dvj += mm(pb, cp)
-                dkj += mm(sg, qp)
-                ot = mm(vt, pb)
-                qt = mm(kt, sg) * SCALE
-                for h in range(2):
-                    part = slice(h * HEAD_DIM, (h + 1) * HEAD_DIM)
-                    ov[:, at[h]] = ot[:, part].T.astype(BF)
-                    dqv[:, at[h]] = qt[:, part].T.astype(BF)
             dpart[0, gi, :, :, lcol] = dvj.reshape(back + 1, tok, HEAD_DIM)
-            dpart[1, gi, :, :, lcol] = (dkj * SCALE).reshape(back + 1, tok, HEAD_DIM)
-            return carry
-
-        lax.fori_loop(0, heads_per, one, 0)
-        wide = heads_per * GROUP * HEAD_DIM
-        mine = pl.ds(gi * wide, wide)
-        for index, (a, b) in enumerate(((ov, out), (dqv, dq))):
-            copy = pltpu.make_async_copy(a.at[:, mine], b.at[:, mine], osem.at[gi, index])
-            copy.start()
-            pending.append((None, copy))
+        grad_step(0, gi, 0)
+
+    def through(j):
+        gi, jl = divmod(j, heads_per)
+        if jl == 0:
+            value_land(gi, back)
+        lcol = slice(jl * HEAD_DIM, (jl + 1) * HEAD_DIM)
+        kt = kwin[gi, :, :, lcol].reshape(window, HEAD_DIM).T
+        vj = vwin[gi, :, :, lcol].reshape(window, HEAD_DIM)
+        vt = vj.T
+        dkj = jnp.zeros((window, HEAD_DIM), F32)
+        for pair in range(GROUP // 2):
+            at, qp, cp = pair_rows(j, pair)
+            pb = probs[j, pair]
+            p = pb.astype(F32)
+            dp = mm(vj, cp, NT)
+            delta = jnp.sum(p * dp, axis=0, keepdims=True)
+            sg = (p * (dp - delta)).astype(BF)
+            dkj += mm(sg, qp)
+            ot = mm(vt, pb)
+            qt = mm(kt, sg) * SCALE
+            for h in range(2):
+                part = slice(h * HEAD_DIM, (h + 1) * HEAD_DIM)
+                ov[:, at[h]] = ot[:, part].T.astype(BF)
+                dqv[:, at[h]] = qt[:, part].T.astype(BF)
+        dpart[1, gi, :, :, lcol] = (dkj * SCALE).reshape(back + 1, tok, HEAD_DIM)
+        if jl == heads_per - 1:
+            grad_step(1, gi, 0)
+            wide = heads_per * GROUP * HEAD_DIM
+            mine = pl.ds(gi * wide, wide)
+            for index, (a, b) in enumerate(((ov, out), (dqv, dq))):
+                copy = pltpu.make_async_copy(a.at[:, mine], b.at[:, mine], osem.at[gi, index])
+                copy.start()
+                pending.append((None, copy))
 
     def grad_copy(w, gi, i):
         return remote(
@@ -260,6 +287,8 @@
         start(remote(
             dvall.at[gi, k, c], dvall.at[gi, k, c], fs.at[gi, 0], gr.at[gi, k, c], dp=partner
         ))
+
+    def key_grads(gi):
         grad_step(1, gi, back)
         dk[:, gi * cols:(gi + 1) * cols] = dpart[1, gi, back].astype(BF)
 
@@ -337,6 +366,11 @@
         copy.start()
         pending.append((None, copy))
 
+    def block(p):
+        if depth % 128 == 0:
+            return ig.at[:, pl.ds(pl.multiple_of(p * depth, 128), depth)]
+        return ig.at[p]
+
     def input_grad(gi):
         rows = dvall[gi].reshape(n * tok, cols)
         got = mm(rows, wv[:, gi * cols:(gi + 1) * cols], NT)
@@ -349,29 +383,22 @@
             for off in range(1, n):
                 p = lax.rem(d + off, n)
                 start(remote(
-                    igs.at[lax.rem(p, 2), lax.div(p, 2)], ig.at[k, c],
+                    igs.at[lax.rem(p, 2), lax.div(p, 2)], block(d),
                     igss.at[off], igr.at[k, c], dp=p,
                 ))
-            copy = pltpu.make_async_copy(igs.at[k, c], ig.at[k, c], loc.at[5])
+            copy = pltpu.make_async_copy(igs.at[k, c], block(d), loc.at[4])
             copy.start()
             pending.append((None, copy))
 
-    for gi in range(PARTS):
-        values_done(gi)
-    local[2].wait()
-    local[3].wait()
-    local[4].wait()
-    key_land(back)
-
-    def grads_start(gi):
-        attention(gi)
-        grad_step(0, gi, 0)
-        grad_step(1, gi, 0)
-
-    def grads_on(gi):
+    def grads_on(w, gi):
         for i in range(1, back):
-            grad_step(0, gi, i)
-            grad_step(1, gi, i)
+            grad_step(w, gi, i)
+
+    def value_grads_on(gi):
+        grads_on(0, gi)
+
+    def key_grads_on(gi):
+        grads_on(1, gi)
 
     def reduces(gi):
         for r in range(AR_CUTS):
@@ -381,16 +408,47 @@
         for r in range(AR_CUTS):
             reduce_out(gi, r)
 
-    stages = [values_on, grads_start, grads_on, gather_send, gather_on, weight_grad, input_grad, reduces, finish]
-    for t in range(PARTS + len(stages) - 1):
-        for s in range(len(stages)):
-            if 0 <= t - s < PARTS:
-                stages[s](t - s)
+    def later(*rows):
+        for row in rows:
+            for at in range(0, len(row), 2):
+                row[at](row[at + 1])
+
+    local[2].wait()
+    local[3].wait()
+    later(
+        (keys_on, 0, keys_on, 1, keys_on, 2),
+        (scores, 0, keys_on, 3),
+        (scores, 1, value_grads_on, 0),
+        (scores, 2, value_grads_on, 1, gather_send, 0),
+        (scores, 3, value_grads_on, 2, gather_send, 1),
+    )
+    values_pair()
+    later((value_grads_on, 3, gather_send, 2))
+    values_own()
+    later((gather_send, 3))
+    for gi in range(PARTS):
+        values_send(gi)
+    turn_hidden()
+    later(
+        (gather_on, 0, gather_on, 1, weight_grad, 0),
+        (gather_on, 2, weight_grad, 1, reduces, 0),
+        (gather_on, 3, weight_grad, 2, reduces, 1, finish, 0),
+        (values_done, 0, weight_grad, 3, reduces, 2, finish, 1),
+        (values_done, 1, values_on, 0, reduces, 3),
+        (values_done, 2, values_on, 1),
+        (values_done, 3, values_on, 2),
+        (input_grad, 0, input_grad, 1, input_grad, 2, input_grad, 3),
+        (through, 0, values_on, 3, finish, 2),
+        (through, 1, through, 2, finish, 3, key_grads_on, 0),
+        (through, 3, through, 4, key_grads_on, 1, key_grads, 0),
+        (through, 5, through, 6, key_grads_on, 2, key_grads, 1),
+        (through, 7, key_grads, 2, key_grads_on, 3, key_grads, 3),
+    )
 
     for off in range(1, n):
         p = lax.rem(d + off, n)
         slot = (lax.rem(p, 2), lax.div(p, 2))
-        remote(igs.at[slot], ig.at[slot], igss.at[0], igr.at[slot], dp=d).wait_recv()
+        remote(igs.at[slot], block(p), igss.at[0], igr.at[slot], dp=d).wait_recv()
     for cond, copy in pending:
         if hasattr(copy, "wait_send") and copy.is_remote:
             when(cond, lambda copy=copy: copy.wait_send())
@@ -406,11 +464,9 @@
     chips = n // 2
     packed = tok * seq
     back = -(-(packed // 2 - 1) // tok)
-    ends = jnp.cumsum(lengths[0])[:-1]
-    at = lax.axis_index("seq") * tok + jnp.arange(tok, dtype=jnp.int32)
-    first = jnp.max(jnp.where(ends[:, None] <= at[None, :], ends[:, None], 0), axis=0)[None, :]
     hid = hidden_states
-    if depth % 128:
+    aligned = depth % 128 == 0
+    if not aligned:
         hid = hid.reshape(tok, n, depth).transpose(1, 0, 2)
     vmem = pl.BlockSpec(memory_space=pltpu.VMEM)
     hbm = pl.BlockSpec(memory_space=pl.ANY)
@@ -421,10 +477,10 @@
             jax.ShapeDtypeStruct(query_states.shape, BF),
             jax.ShapeDtypeStruct(query_states.shape, BF),
             jax.ShapeDtypeStruct(key_states.shape, BF),
-            jax.ShapeDtypeStruct((2, chips, tok, depth), BF),
+            jax.ShapeDtypeStruct((tok, width) if aligned else (n, tok, depth), BF),
             jax.ShapeDtypeStruct((depth, kv_cols), F32),
         ),
-        in_specs=[vmem, hbm, hbm, hbm, hbm, hbm],
+        in_specs=[pl.BlockSpec(memory_space=pltpu.SMEM), hbm, hbm, hbm, hbm, hbm],
         out_specs=(hbm, hbm, vmem, hbm, hbm),
         scratch_shapes=[
             pltpu.VMEM((2, chips, tok, depth), BF),
@@ -434,8 +490,9 @@
             pltpu.VMEM(query_states.shape, BF),
             pltpu.VMEM(query_states.shape, BF),
             pltpu.VMEM(query_states.shape, BF),
-            pltpu.VMEM((back + 1, tok, kv_cols), BF),
             pltpu.VMEM((PARTS, back + 1, tok, cols), BF),
+            pltpu.VMEM((PARTS, back + 1, tok, cols), BF),
+            pltpu.VMEM((KV_HEADS, GROUP // 2, (back + 1) * tok, 2 * tok), BF),
             pltpu.VMEM((PARTS, 2, chips, tok, cols), BF),
             pltpu.VMEM((PARTS, chips, tok, cols), BF),
             pltpu.VMEM((PARTS, chips, tok, cols), BF),
@@ -451,9 +508,9 @@
             pltpu.VMEM((PARTS, depth, cols), BF),
             pltpu.VMEM((PARTS, depth, cols), BF),
             pltpu.VMEM((PARTS, depth, cols), BF),
-            dma((6,)),
+            dma((5 + PARTS,)),
             dma((n,)), dma((2, chips)),
-            dma((back,)), dma((back,)),
+            dma((PARTS, back)), dma((PARTS, back)),
             dma((PARTS,)), dma((PARTS,)),
             dma((PARTS, chips)), dma((PARTS, chips)),
             dma((PARTS, back)), dma((PARTS, back)),
@@ -468,9 +525,10 @@
         compiler_params=pltpu.CompilerParams(
             collective_id=0, has_side_effects=True, vmem_limit_bytes=60 * 1024 * 1024
         ),
-    )(first, hid, value_weight, query_states, key_states, cotangent)
-    input_grad = ig.transpose(2, 1, 0, 3).reshape(tok, width)
-    return out, dq, dk, input_grad, dw
+    )(lengths, hid, value_weight, query_states, key_states, cotangent)
+    if not aligned:
+        ig = ig.transpose(1, 0, 2).reshape(tok, width)
+    return out, dq, dk, ig, dw
 
 
 def solution(mesh):

time: 127 us -> 126 us (level)
  Pallas kernels: 115 us -> 117 us
  local copies, waits for them, and re-layouts: 9.9 us -> 8.07 us
  other arithmetic: 1.43 us -> 0 us
    pallas_call x1, Pallas kernels: 115 us -> 117 us  [body(): pl.pallas_call(functools.partial(kernel, n, seq, back, tok, depth), out_s...]
    transpose x1 -> x0, local copies, waits for them, and re-layouts: 1.92 us -> none  [body(): input_grad = ig.transpose(2, 1, 0, 3).reshape(tok, width)]
where the time goes in v1:
time: 126 us
  Pallas kernels  117 us (93%)
  local copies, waits for them, and re-layouts  8.07 us (6%)
    pallas_call x1, Pallas kernels, body(): pl.pallas_call(functools.partial(kernel, n, seq, back, tok, depth), out_s...  117 us
    unnamed x13, local copies, waits for them, and re-layouts  8.07 us

profile of v1, /device:TPU:0, one launch (start us, length us, event | category | flops | bytes accessed | tf_op | source)
XLA Modules:
  0.0 126.2 jit_solution(9946503256176125685)
XLA Ops:
  0.6 117.5 %shard_map.101 = (bf16[128,8192]{1,0:T(8,128)(2,1)}, bf16[128,8192]{1,0:T(8,128)(2,1)}, bf16[128,1024]{1,0:T(8,128)(2,1)}, bf16[128,5120]{1,0:T(8,128)(2,1)}, f32[640,1024]{1,0:T(8,128)}) custom-call(s32[1,8]{1,0:T(1,128)} %lengths.1, bf16[128,5120]{1,0:T(8,128)(2,1)} %hid.1, bf16[640,1024]{1,0:T(8,128)(2,1)} %weight.1, bf16[128,8192]{1,0:T(8,128)(2,1)} %query.1, ...), custom_call_target="tpu_custom_call" | custom-call | tf_op jit(solution)/shard_map/pallas_call | solution.py:474
  118.1 0.0 copy-start.1
  118.1 3.2 %copy.16 = bf16[128,8192]{1,0:T(8,128)(2,1)} copy(bf16[128,8192]{1,0:T(8,128)(2,1)} %get-tuple-element.10) | data formatting | bytes 4194304
  121.3 0.0 copy-done.1
  121.3 0.0 copy-start.3
  121.4 0.0 copy-start.2
  121.4 1.3 %copy.17 = bf16[128,8192]{1,0:T(8,128)(2,1)} copy(bf16[128,8192]{1,0:T(8,128)(2,1)S(1)} %copy-done.1) | data formatting | bytes 4194304
  122.7 0.0 copy-done.3
  122.7 0.0 copy-start
  122.7 0.7 copy.18
  123.4 0.1 copy-done.2
  123.5 1.1 copy.19
  124.6 0.1 copy-done
  124.7 1.5 %copy.20 = f32[640,1024]{1,0:T(8,128)} copy(f32[640,1024]{1,0:T(8,128)S(1)} %copy-done) | data formatting | bytes 5242880
Async XLA Ops:
  118.1 3.3 %copy-start.1 = (bf16[128,8192]{1,0:T(8,128)(2,1)S(1)}, bf16[128,8192]{1,0:T(8,128)(2,1)}, u32[]{:S(2)}) copy-start(bf16[128,8192]{1,0:T(8,128)(2,1)} %get-tuple-element.11) | copy-start | bytes 6291460
  121.3 1.3 %copy-start.3 = (bf16[128,1024]{1,0:T(8,128)(2,1)S(1)}, bf16[128,1024]{1,0:T(8,128)(2,1)}, u32[]{:S(2)}) copy-start(bf16[128,1024]{1,0:T(8,128)(2,1)} %get-tuple-element.12) | copy-start | bytes 786436
  121.4 2.2 %copy-start.2 = (bf16[128,5120]{1,0:T(8,128)(2,1)S(1)}, bf16[128,5120]{1,0:T(8,128)(2,1)}, u32[]{:S(2)}) copy-start(bf16[128,5120]{1,0:T(8,128)(2,1)} %get-tuple-element.13) | copy-start | bytes 3932164
  122.7 2.0 %copy-start = (f32[640,1024]{1,0:T(8,128)S(1)}, f32[640,1024]{1,0:T(8,128)}, u32[]{:S(2)}) copy-start(f32[640,1024]{1,0:T(8,128)} %get-tuple-element.14) | copy-start | bytes 7864324

commit v2 on v1

--- a/solution.py
+++ b/solution.py
@@ -245,12 +245,12 @@
             delta = jnp.sum(p * dp, axis=0, keepdims=True)
             sg = (p * (dp - delta)).astype(BF)
             dkj += mm(sg, qp)
-            ot = mm(vt, pb)
-            qt = mm(kt, sg) * SCALE
+            ot = mm(vt, pb).astype(BF)
+            qt = (mm(kt, sg) * SCALE).astype(BF)
             for h in range(2):
                 part = slice(h * HEAD_DIM, (h + 1) * HEAD_DIM)
-                ov[:, at[h]] = ot[:, part].T.astype(BF)
-                dqv[:, at[h]] = qt[:, part].T.astype(BF)
+                ov[:, at[h]] = ot[:, part].T
+                dqv[:, at[h]] = qt[:, part].T
         dpart[1, gi, :, :, lcol] = (dkj * SCALE).reshape(back + 1, tok, HEAD_DIM)
         if jl == heads_per - 1:
             grad_step(1, gi, 0)
@@ -419,30 +419,27 @@
         (keys_on, 0, keys_on, 1, keys_on, 2),
         (scores, 0, keys_on, 3),
         (scores, 1, value_grads_on, 0),
-        (scores, 2, value_grads_on, 1, gather_send, 0),
-        (scores, 3, value_grads_on, 2, gather_send, 1),
     )
     values_pair()
-    later((value_grads_on, 3, gather_send, 2))
+    later((scores, 2, value_grads_on, 1, gather_send, 0))
     values_own()
-    later((gather_send, 3))
     for gi in range(PARTS):
         values_send(gi)
+    later((scores, 3, value_grads_on, 2, gather_send, 1))
     turn_hidden()
     later(
-        (gather_on, 0, gather_on, 1, weight_grad, 0),
-        (gather_on, 2, weight_grad, 1, reduces, 0),
-        (gather_on, 3, weight_grad, 2, reduces, 1, finish, 0),
-        (values_done, 0, weight_grad, 3, reduces, 2, finish, 1),
-        (values_done, 1, values_on, 0, reduces, 3),
-        (values_done, 2, values_on, 1),
-        (values_done, 3, values_on, 2),
+        (value_grads_on, 3, gather_send, 2, values_done, 0, gather_send, 3),
+        (values_done, 1, gather_on, 0, values_on, 0, values_done, 2, values_on, 1),
+        (weight_grad, 0, gather_on, 1, through, 0),
+        (values_done, 3, values_on, 2, weight_grad, 1, gather_on, 2, through, 1),
+        (values_on, 3, reduces, 0, weight_grad, 2, gather_on, 3, through, 2),
+        (reduces, 1, weight_grad, 3),
         (input_grad, 0, input_grad, 1, input_grad, 2, input_grad, 3),
-        (through, 0, values_on, 3, finish, 2),
-        (through, 1, through, 2, finish, 3, key_grads_on, 0),
-        (through, 3, through, 4, key_grads_on, 1, key_grads, 0),
-        (through, 5, through, 6, key_grads_on, 2, key_grads, 1),
-        (through, 7, key_grads, 2, key_grads_on, 3, key_grads, 3),
+        (through, 3, finish, 0, reduces, 2, through, 4),
+        (finish, 1, reduces, 3, through, 5, key_grads_on, 0, through, 6),
+        (finish, 2, key_grads_on, 1, through, 7),
+        (key_grads_on, 2, key_grads, 0, finish, 3, key_grads_on, 3),
+        (key_grads, 1, key_grads, 2, key_grads, 3),
     )
 
     for off in range(1, n):

time: 126 us -> 109 us (0.87)
  Pallas kernels: 117 us -> 100 us
    pallas_call x1, Pallas kernels: 117 us -> 100 us  [body(): pl.pallas_call(functools.partial(kernel, n, seq, back, tok, depth), out_s...]
where the time goes in v2:
time: 109 us
  Pallas kernels  100 us (92%)
  local copies, waits for them, and re-layouts  8.07 us (7%)
    pallas_call x1, Pallas kernels, body(): pl.pallas_call(functools.partial(kernel, n, seq, back, tok, depth), out_s...  100 us
    unnamed x13, local copies, waits for them, and re-layouts  8.07 us

profile of v2, /device:TPU:0, one launch (start us, length us, event | category | flops | bytes accessed | tf_op | source)
XLA Modules:
  0.0 108.9 jit_solution(9994947399976737722)
XLA Ops:
  0.6 100.2 %shard_map.101 = (bf16[128,8192]{1,0:T(8,128)(2,1)}, bf16[128,8192]{1,0:T(8,128)(2,1)}, bf16[128,1024]{1,0:T(8,128)(2,1)}, bf16[128,5120]{1,0:T(8,128)(2,1)}, f32[640,1024]{1,0:T(8,128)}) custom-call(s32[1,8]{1,0:T(1,128)} %lengths.1, bf16[128,5120]{1,0:T(8,128)(2,1)} %hid.1, bf16[640,1024]{1,0:T(8,128)(2,1)} %weight.1, bf16[128,8192]{1,0:T(8,128)(2,1)} %query.1, ...), custom_call_target="tpu_custom_call" | custom-call | tf_op jit(solution)/shard_map/pallas_call | solution.py:471
  100.9 0.0 copy-start.1
  100.9 3.2 %copy.16 = bf16[128,8192]{1,0:T(8,128)(2,1)} copy(bf16[128,8192]{1,0:T(8,128)(2,1)} %get-tuple-element.10) | data formatting | bytes 4194304
  104.1 0.0 copy-done.1
  104.1 0.0 copy-start.3
  104.1 0.0 copy-start.2
  104.1 1.3 %copy.17 = bf16[128,8192]{1,0:T(8,128)(2,1)} copy(bf16[128,8192]{1,0:T(8,128)(2,1)S(1)} %copy-done.1) | data formatting | bytes 4194304
  105.4 0.0 copy-done.3
  105.4 0.0 copy-start
  105.4 0.7 copy.18
  106.2 0.1 copy-done.2
  106.3 1.1 copy.19
  107.3 0.1 copy-done
  107.5 1.5 %copy.20 = f32[640,1024]{1,0:T(8,128)} copy(f32[640,1024]{1,0:T(8,128)S(1)} %copy-done) | data formatting | bytes 5242880
Async XLA Ops:
  100.9 3.3 %copy-start.1 = (bf16[128,8192]{1,0:T(8,128)(2,1)S(1)}, bf16[128,8192]{1,0:T(8,128)(2,1)}, u32[]{:S(2)}) copy-start(bf16[128,8192]{1,0:T(8,128)(2,1)} %get-tuple-element.11) | copy-start | bytes 6291460
  104.1 1.3 %copy-start.3 = (bf16[128,1024]{1,0:T(8,128)(2,1)S(1)}, bf16[128,1024]{1,0:T(8,128)(2,1)}, u32[]{:S(2)}) copy-start(bf16[128,1024]{1,0:T(8,128)(2,1)} %get-tuple-element.12) | copy-start | bytes 786436
  104.1 2.2 %copy-start.2 = (bf16[128,5120]{1,0:T(8,128)(2,1)S(1)}, bf16[128,5120]{1,0:T(8,128)(2,1)}, u32[]{:S(2)}) copy-start(bf16[128,5120]{1,0:T(8,128)(2,1)} %get-tuple-element.13) | copy-start | bytes 3932164
  105.4 2.0 %copy-start = (f32[640,1024]{1,0:T(8,128)S(1)}, f32[640,1024]{1,0:T(8,128)}, u32[]{:S(2)}) copy-start(f32[640,1024]{1,0:T(8,128)} %get-tuple-element.14) | copy-start | bytes 7864324

commit v3 on v2

--- a/solution.py
+++ b/solution.py
@@ -429,15 +429,13 @@
     turn_hidden()
     later(
         (value_grads_on, 3, gather_send, 2, values_done, 0, gather_send, 3),
-        (values_done, 1, gather_on, 0, values_on, 0, values_done, 2, values_on, 1),
-        (weight_grad, 0, gather_on, 1, through, 0),
-        (values_done, 3, values_on, 2, weight_grad, 1, gather_on, 2, through, 1),
-        (values_on, 3, reduces, 0, weight_grad, 2, gather_on, 3, through, 2),
-        (reduces, 1, weight_grad, 3),
+        (gather_on, 0, weight_grad, 0, values_done, 1, values_on, 0, values_done, 2, values_on, 1),
+        (through, 0, gather_on, 1, weight_grad, 1, values_done, 3, values_on, 2),
+        (through, 1, reduces, 0, gather_on, 2, weight_grad, 2, values_on, 3),
+        (through, 2, reduces, 1, gather_on, 3, weight_grad, 3),
         (input_grad, 0, input_grad, 1, input_grad, 2, input_grad, 3),
-        (through, 3, finish, 0, reduces, 2, through, 4),
-        (finish, 1, reduces, 3, through, 5, key_grads_on, 0, through, 6),
-        (finish, 2, key_grads_on, 1, through, 7),
+        (reduces, 2, through, 3, finish, 0, reduces, 3, through, 4, finish, 1),
+        (through, 5, key_grads_on, 0, through, 6, finish, 2, key_grads_on, 1, through, 7),
         (key_grads_on, 2, key_grads, 0, finish, 3, key_grads_on, 3),
         (key_grads, 1, key_grads, 2, key_grads, 3),
     )

time: 109 us -> 114 us (1.046)
  Pallas kernels: 100 us -> 105 us
    pallas_call x1, Pallas kernels: 100 us -> 105 us  [body(): pl.pallas_call(functools.partial(kernel, n, seq, back, tok, depth), out_s...]
where the time goes in v3:
time: 114 us; the launch traced here: 113 us
  Pallas kernels  105 us (92%)
  local copies, waits for them, and re-layouts  8.07 us (7%)
    pallas_call x1, Pallas kernels, body(): pl.pallas_call(functools.partial(kernel, n, seq, back, tok, depth), out_s...  105 us
    unnamed x13, local copies, waits for them, and re-layouts  8.07 us

profile of v3, /device:TPU:0, one launch (start us, length us, event | category | flops | bytes accessed | tf_op | source)
XLA Modules:
  0.0 113.4 jit_solution(1946057809249372331)
XLA Ops:
  0.6 104.7 %shard_map.101 = (bf16[128,8192]{1,0:T(8,128)(2,1)}, bf16[128,8192]{1,0:T(8,128)(2,1)}, bf16[128,1024]{1,0:T(8,128)(2,1)}, bf16[128,5120]{1,0:T(8,128)(2,1)}, f32[640,1024]{1,0:T(8,128)}) custom-call(s32[1,8]{1,0:T(1,128)} %lengths.1, bf16[128,5120]{1,0:T(8,128)(2,1)} %hid.1, bf16[640,1024]{1,0:T(8,128)(2,1)} %weight.1, bf16[128,8192]{1,0:T(8,128)(2,1)} %query.1, ...), custom_call_target="tpu_custom_call" | custom-call | tf_op jit(solution)/shard_map/pallas_call | solution.py:469
  105.3 0.0 copy-start.1
  105.4 3.2 %copy.16 = bf16[128,8192]{1,0:T(8,128)(2,1)} copy(bf16[128,8192]{1,0:T(8,128)(2,1)} %get-tuple-element.10) | data formatting | bytes 4194304
  108.6 0.0 copy-done.1
  108.6 0.0 copy-start.3
  108.6 0.0 copy-start.2
  108.6 1.3 %copy.17 = bf16[128,8192]{1,0:T(8,128)(2,1)} copy(bf16[128,8192]{1,0:T(8,128)(2,1)S(1)} %copy-done.1) | data formatting | bytes 4194304
  109.9 0.0 copy-done.3
  109.9 0.0 copy-start
  109.9 0.7 copy.18
  110.6 0.1 copy-done.2
  110.8 1.1 copy.19
  111.8 0.1 copy-done
  111.9 1.5 %copy.20 = f32[640,1024]{1,0:T(8,128)} copy(f32[640,1024]{1,0:T(8,128)S(1)} %copy-done) | data formatting | bytes 5242880
Async XLA Ops:
  105.3 3.3 %copy-start.1 = (bf16[128,8192]{1,0:T(8,128)(2,1)S(1)}, bf16[128,8192]{1,0:T(8,128)(2,1)}, u32[]{:S(2)}) copy-start(bf16[128,8192]{1,0:T(8,128)(2,1)} %get-tuple-element.11) | copy-start | bytes 6291460
  108.6 1.3 %copy-start.3 = (bf16[128,1024]{1,0:T(8,128)(2,1)S(1)}, bf16[128,1024]{1,0:T(8,128)(2,1)}, u32[]{:S(2)}) copy-start(bf16[128,1024]{1,0:T(8,128)(2,1)} %get-tuple-element.12) | copy-start | bytes 786436
  108.6 2.2 %copy-start.2 = (bf16[128,5120]{1,0:T(8,128)(2,1)S(1)}, bf16[128,5120]{1,0:T(8,128)(2,1)}, u32[]{:S(2)}) copy-start(bf16[128,5120]{1,0:T(8,128)(2,1)} %get-tuple-element.13) | copy-start | bytes 3932164
  109.9 2.0 %copy-start = (f32[640,1024]{1,0:T(8,128)S(1)}, f32[640,1024]{1,0:T(8,128)}, u32[]{:S(2)}) copy-start(f32[640,1024]{1,0:T(8,128)} %get-tuple-element.14) | copy-start | bytes 7864324
